TPU v7x, 32 devices: a whole 2x2x4 slice. The times are simulated.
32 devices in a mesh: slab: 2 (over y), gx: 4 (over x, core), gy: 4 (over z).
Axes of the slice: x: 2, y: 2, z: 4, core: 2. Of those that a mesh axis runs over, the one named last changes fastest.
Arguments:
- slab_feature_entries: bfloat16 [64, 32, 8, 512], P(('slab', 'gx'), 'gy'), parts along dimension 0, may hold values from -6 to 6
- depthwise_filter_coefficients: float32 [27, 512], replicated, may hold values from -1.2 to 1.2
- rootmean_scaling_factors: float32 [512], replicated, may hold values from 0.5 to 1.5
- asking_projection_factors: bfloat16 [512, 512], replicated, may hold values from -0.25 to 0.25
- lookup_projection_factors: bfloat16 [512, 512], replicated, may hold values from -0.25 to 0.25
- content_projection_factors: bfloat16 [512, 512], replicated, may hold values from -0.25 to 0.25
- final_projection_factors: bfloat16 [512, 512], replicated, may hold values from -0.25 to 0.25
- softness_per_attender: float32 [8], replicated, may hold values from 4 to 16
- adjacent_block_codes: int32 [16, 8, 2, 7], P(('slab', 'gx'), 'gy'), parts along dimension 0, may hold values from 0 to 6, as said below
- filled_list_lengths: int32 [16, 8, 2], P(('slab', 'gx'), 'gy'), parts along dimension 0, may hold values from 1 to 7, as said below
Outputs:
- mixed: bfloat16 [64, 32, 8, 512], P(('slab', 'gx'), 'gy'), parts along dimension 0
There are 2 independent parts, one for each index of `slab`. A program takes and returns all parts, laid end to end along the dimension named above; an argument that names none is the same for every part. Nothing has to cross between parts.
Inputs may be any that keep to these rules, and one draw needn't show every extreme that they name: `adjacent_block_codes`: every list starts with 0 and holds 7 distinct codes; entries past filled_list_lengths are present but unused. `filled_list_lengths`: some block of every slab uses all 7 entries and some block uses only the first.
All inputs are finite; a program needn't handle non-finite values.
Results may differ from a plain program's by a relative error of at most 0.0075.
Values may be sent and summed in bfloat16 or wider, within the bound.
A program may use at most 128 MiB of HBM per device.

v0:
```python
import math

import jax
import jax.numpy as jnp
from jax import lax
from jax.experimental import pallas as pl
from jax.experimental.pallas import tpu as pltpu
from jax.sharding import PartitionSpec as P

BLOCK = 4
MESH = pl.DeviceIdType.MESH
F32 = jnp.float32
BF16 = jnp.bfloat16


def kernel(
    count_gx,
    count_gy,
    x_hbm,
    taps_hbm,
    gain_hbm,
    wq_hbm,
    wk_hbm,
    wv_hbm,
    wf_hbm,
    soft_hbm,
    codes_hbm,
    lens_hbm,
    out_hbm,
    out_ref,
    x_ref,
    taps_ref,
    gain_ref,
    wq_ref,
    wk_ref,
    wv_ref,
    wf_ref,
    soft_ref,
    codes_ref,
    lens_ref,
    framed,
    summed,
    rim_x,
    rim_y,
    rim_c,
    hidden,
    normed,
    near_x,
    near_y,
    query,
    key,
    value,
    key_x,
    value_x,
    key_y,
    value_y,
    acc,
    tot,
    send_sem,
    recv_sem,
    load_sem,
    store_sem,
):
    operands = (
        (x_hbm, x_ref),
        (taps_hbm, taps_ref),
        (gain_hbm, gain_ref),
        (wk_hbm, wk_ref),
        (wv_hbm, wv_ref),
        (wq_hbm, wq_ref),
        (soft_hbm, soft_ref),
        (codes_hbm, codes_ref),
        (lens_hbm, lens_ref),
        (wf_hbm, wf_ref),
    )
    loads = [
        pltpu.make_async_copy(src, dst, load_sem.at[i]) for i, (src, dst) in enumerate(operands)
    ]
    for load in loads:
        load.start()
    gx = lax.axis_index("gx")
    gy = lax.axis_index("gy")
    has_x = (gx > 0, gx < count_gx - 1)
    has_y = (gy > 0, gy < count_gy - 1)
    step = (-1, 1)

    def target(dx, dy):
        return {"gx": gx + dx, "gy": gy + dy}

    def exists(dx, dy):
        conds = []
        if dx:
            conds.append(has_x[(dx + 1) // 2])
        if dy:
            conds.append(has_y[(dy + 1) // 2])
        return conds[0] if len(conds) == 1 else conds[0] & conds[1]

    around = [(dx, dy) for dx in (-1, 0, 1) for dy in (-1, 0, 1) if dx or dy]

    barrier = pltpu.get_barrier_semaphore()
    for dx, dy in around:

        @pl.when(exists(dx, dy))
        def _():
            pl.semaphore_signal(barrier, inc=1, device_id=target(dx, dy), device_id_type=MESH)

    span_x = 1 + has_x[0].astype(jnp.int32) + has_x[1].astype(jnp.int32)
    span_y = 1 + has_y[0].astype(jnp.int32) + has_y[1].astype(jnp.int32)
    pl.semaphore_wait(barrier, span_x * span_y - 1)

    def copy(src, dst, out_slot, in_slot, dx, dy):
        return pltpu.make_async_remote_copy(
            src_ref=src,
            dst_ref=dst,
            send_sem=send_sem.at[out_slot],
            recv_sem=recv_sem.at[in_slot],
            device_id=target(dx, dy),
            device_id_type=MESH,
        )

    rims = []
    landing = {}
    for side in (0, 1):
        other = 1 - side
        edge = 7 * side
        rims.append((step[side], 0, x_hbm.at[edge], rim_x.at[other], side, other))
        rims.append((0, step[side], x_hbm.at[:, edge], rim_y.at[other], 2 + side, 2 + other))
        landing[side] = (step[side], 0, rim_x.at[side])
        landing[2 + side] = (0, step[side], rim_y.at[side])
        for side_y in (0, 1):
            at = 2 * side + side_y
            rims.append(
                (
                    step[side],
                    step[side_y],
                    x_hbm.at[edge, 7 * side_y],
                    rim_c.at[3 - at],
                    4 + at,
                    4 + 3 - at,
                )
            )
            landing[4 + at] = (step[side], step[side_y], rim_c.at[at])
    faces = ([], [])
    for half in (0, 1):
        for side in (0, 1):
            other = 1 - side
            faces[half].append(
                (
                    0,
                    step[side],
                    normed.at[half, side],
                    near_y.at[other, half],
                    10 + 2 * side + half,
                    10 + 2 * other + half,
                )
            )
            landing[10 + 2 * side + half] = (0, step[side], near_y.at[side, half])
        faces[half].append(
            (step[half], 0, normed.at[half], near_x.at[1 - half], 8 + half, 8 + 1 - half)
        )
        landing[8 + half] = (step[half], 0, near_x.at[half])

    def start(item):
        dx, dy, src, dst, out_slot, in_slot = item

        @pl.when(exists(dx, dy))
        def _():
            copy(src, dst, out_slot, in_slot, dx, dy).start()

    def finish_send(item):
        dx, dy, src, dst, out_slot, in_slot = item

        @pl.when(exists(dx, dy))
        def _():
            copy(src, dst, out_slot, in_slot, dx, dy).wait_send()

    def arrive(slot, landed, absent):
        dx, dy, buffer = landing[slot]

        @pl.when(exists(dx, dy))
        def _():
            copy(buffer, buffer, slot, slot, dx, dy).wait_recv()
            if landed is not None:
                landed()

        @pl.when(jnp.logical_not(exists(dx, dy)))
        def _():
            absent()

    for item in rims:
        start(item)

    for load in loads[:3]:
        load.wait()

    for at in (0, 9):
        framed[at] = jnp.zeros((10, 8, 512), F32)
        framed[:, at] = jnp.zeros((10, 8, 512), F32)

    @pl.loop(0, 8)
    def _(x):
        framed[x + 1, 1:9] = x_ref[x].astype(F32)

    def add_taps(pieces, lanes):
        sums = [None, None, None]
        for a, b, piece in pieces:
            for c in range(3):
                tap = 9 * a + 3 * b + c
                coefficient = taps_ref[tap : tap + 1, lanes]
                if piece.ndim == 3:
                    coefficient = coefficient.reshape(1, 1, 128)
                term = piece * coefficient
                sums[c] = term if sums[c] is None else sums[c] + term
        axis = sums[0].ndim - 2
        depth_at = lax.broadcasted_iota(jnp.int32, sums[0].shape, axis)
        low = jnp.where(depth_at > 0, pltpu.roll(sums[0], 1, axis), 0.0)
        high = jnp.where(depth_at < 7, pltpu.roll(sums[2], 7, axis), 0.0)
        return sums[1] + low + high

    groups = [slice(128 * group, 128 * group + 128) for group in range(4)]

    @pl.loop(0, 8)
    def _(x):
        for lanes in groups:
            pieces = [
                (a, b, framed[x + a, b : b + 8, :, lanes]) for a in range(3) for b in range(3)
            ]
            own = framed[x + 1, 1:9, :, lanes]
            summed[x, :, :, lanes] = own + add_taps(pieces, lanes)

    def fill(index, ref):
        def landed():
            framed[index] = ref[...].astype(F32)

        return landed, lambda: None

    for side in (0, 1):
        at = 9 * side
        arrive(side, *fill((at, slice(1, 9)), rim_x.at[side]))
        for lanes in groups:
            pieces = [(2 * side, b, framed[at, b : b + 8, :, lanes]) for b in range(3)]
            summed[7 * side, :, :, lanes] = summed[7 * side, :, :, lanes] + add_taps(pieces, lanes)
    for side in (0, 1):
        at = 9 * side
        arrive(2 + side, *fill((slice(1, 9), at), rim_y.at[side]))
        for side_y in (0, 1):
            arrive(4 + 2 * side + side_y, *fill((at, 9 * side_y), rim_c.at[2 * side + side_y]))

    half_at = lax.broadcasted_iota(jnp.int32, (4, 8, 512), 1) < 4
    gain = gain_ref[...].reshape(1, 1, 512)
    for half in (0, 1):

        @pl.loop(0, 4)
        def _(xi):
            x = 4 * half + xi
            edges = []
            for side in (0, 1):
                parts = []
                for lanes in groups:
                    pieces = [(a, 2 * side, framed[x + a, 9 * side, :, lanes]) for a in range(3)]
                    parts.append(add_taps(pieces, lanes))
                edges.append(jnp.concatenate(parts, axis=-1) + summed[x, 7 * side])
            rows = jnp.concatenate([edges[0][None], summed[x, 1:7], edges[1][None]], axis=0)
            rows = rows.astype(BF16).astype(F32)
            pairs = rows.reshape(4, 2, 8, 512)
            even, odd = pairs[:, 0], pairs[:, 1]
            lower = jnp.where(half_at, even, pltpu.roll(odd, 4, 1))
            upper = jnp.where(half_at, pltpu.roll(even, 4, 1), odd)
            for bz, part in ((0, lower), (1, upper)):
                scale = lax.rsqrt(jnp.mean(part * part, axis=-1, keepdims=True) + 1e-05)
                unit = (part * scale * gain).reshape(2, 16, 512).astype(BF16)
                part = part.reshape(2, 16, 512).astype(BF16)
                for by in (0, 1):
                    hidden[half, by, bz, xi] = part[by]
                    normed[half, by, bz, xi] = unit[by]

        for item in faces[half]:
            start(item)

    for load in loads[3:6]:
        load.wait()
    row = lax.broadcasted_iota(jnp.int32, (256, 256), 0) // 64
    column = lax.broadcasted_iota(jnp.int32, (256, 256), 1) // 64
    same_head = (row == column).astype(F32).astype(BF16)
    head_at = lax.broadcasted_iota(jnp.int32, (64, 256), 1) // 64

    def units(raw):
        values = raw.astype(BF16).astype(F32)
        squares = values * values
        upper = squares.astype(BF16)
        rest = (squares - upper.astype(F32)).astype(BF16)
        sums = jnp.dot(upper, same_head, preferred_element_type=F32)
        sums = sums + jnp.dot(rest, same_head, preferred_element_type=F32)
        return values * lax.rsqrt(sums + 1e-06)

    def project(tokens, w_ref, quad):
        lanes = slice(256 * quad, 256 * quad + 256)
        return jnp.dot(tokens, w_ref[:, lanes], preferred_element_type=F32)

    def keys_values(src, key_dst, value_dst):
        tokens = src[...].reshape(-1, 512)
        shape = key_dst.shape[:-1] + (256,)
        for quad in (0, 1):
            lanes = slice(256 * quad, 256 * quad + 256)
            unit = units(project(tokens, wk_ref, quad)).astype(BF16)
            key_dst[..., lanes] = unit.reshape(shape)
            raw = project(tokens, wv_ref, quad).astype(BF16)
            value_dst[..., lanes] = raw.reshape(shape)

    for half in (0, 1):
        tokens = normed[half].reshape(256, 512)
        for quad in (0, 1):
            unit = units(project(tokens, wq_ref, quad)).reshape(2, 2, 64, 256)
            for by in (0, 1):
                for bz in (0, 1):
                    for j in range(4):
                        kept = jnp.where(head_at == j, unit[by, bz], 0.0)
                        query[half, by, bz, quad, 64 * j : 64 * j + 64] = kept.astype(BF16)
        keys_values(normed.at[half], key.at[half], value.at[half])

    for load in loads[6:]:
        load.wait()
    log2e = math.log2(math.e)
    slots = codes_ref.shape[3]

    def attend(bx, by, bz, near):
        extent = 64 * len(near)
        slot_at = lax.broadcasted_iota(jnp.int32, (1, extent), 1) // 64
        named = jnp.full((1, extent), -2, jnp.int32)
        for j, (code, _, _) in enumerate(near):
            named = jnp.where(slot_at == j, code, named)
        mask = jnp.zeros((1, extent), F32)
        length = lens_ref[bx, by, bz]
        for s in range(slots):
            code = jnp.where(s < length, codes_ref[bx, by, bz, s], -1)
            mask = jnp.where(named == code, 1.0, mask)
        outs, sums = [], []
        for quad in (0, 1):
            lanes = slice(256 * quad, 256 * quad + 256)
            keys = jnp.concatenate([k[..., lanes] for _, k, _ in near], axis=0)
            values = jnp.concatenate([v[..., lanes] for _, _, v in near], axis=0)
            score = lax.dot_general(
                query[bx, by, bz, quad],
                keys,
                (((1,), (1,)), ((), ())),
                preferred_element_type=F32,
            )
            weights, totals = [], []
            for j in range(4):
                factor = soft_ref[4 * quad + j] * log2e
                weight = jnp.exp2(score[64 * j : 64 * j + 64] * factor) * mask
                totals.append(jnp.sum(weight, axis=-1, keepdims=True))
                weights.append(weight.astype(BF16))
            mixed = jnp.dot(
                jnp.concatenate(weights, axis=0), values, preferred_element_type=F32
            )
            out = mixed[0:64]
            total = jnp.broadcast_to(totals[0], (64, 256))
            for j in range(1, 4):
                out = jnp.where(head_at == j, mixed[64 * j : 64 * j + 64], out)
                total = jnp.where(head_at == j, totals[j], total)
            outs.append(out)
            sums.append(total)
        return outs, sums

    def attend_own(bx, by, bz):
        near = [
            (6 * bz, key.at[bx, by, 0], value.at[bx, by, 0]),
            (5 * (1 - bz), key.at[bx, by, 1], value.at[bx, by, 1]),
            (1 + bx, key.at[1 - bx, by, bz], value.at[1 - bx, by, bz]),
            (3 + by, key.at[bx, 1 - by, bz], value.at[bx, 1 - by, bz]),
        ]
        outs, sums = attend(bx, by, bz, near)
        for quad in (0, 1):
            lanes = slice(256 * quad, 256 * quad + 256)
            acc[bx, by, bz, :, lanes] = outs[quad]
            tot[bx, by, bz, :, lanes] = sums[quad]

    @pl.loop(0, 2, unroll=True)
    def _(bx):
        for by in (0, 1):
            for bz in (0, 1):
                attend_own(bx, by, bz)

    for side in (0, 1):

        def empty(ref=near_x.at[side]):
            ref[...] = jnp.zeros(ref.shape, BF16)

        arrive(8 + side, None, empty)
        keys_values(near_x.at[side], key_x.at[side], value_x.at[side])
    for side in (0, 1):
        for half in (0, 1):

            def empty(ref=near_y.at[side, half]):
                ref[...] = jnp.zeros(ref.shape, BF16)

            arrive(10 + 2 * side + half, None, empty)
        keys_values(near_y.at[side], key_y.at[side], value_y.at[side])

    in_x = [has.astype(jnp.int32) for has in has_x]
    in_y = [has.astype(jnp.int32) for has in has_y]

    def attend_near(bx, by, bz):
        inside_x = jnp.where(bx == 0, in_x[0], in_x[1])
        inside_y = jnp.where(by == 0, in_y[0], in_y[1])
        near = [
            (
                jnp.where(inside_x > 0, 2 - bx, -2),
                key_x.at[bx, by, bz],
                value_x.at[bx, by, bz],
            ),
            (
                jnp.where(inside_y > 0, 4 - by, -2),
                key_y.at[by, bx, bz],
                value_y.at[by, bx, bz],
            ),
        ]
        outs, sums = attend(bx, by, bz, near)
        for quad in (0, 1):
            lanes = slice(256 * quad, 256 * quad + 256)
            result = (acc[bx, by, bz, :, lanes] + outs[quad]) / (
                tot[bx, by, bz, :, lanes] + sums[quad]
            )
            query[bx, by, bz, 0, 64 * quad : 64 * quad + 64] = result.astype(BF16)

    @pl.loop(0, 2, unroll=True)
    def _(bx):
        for by in (0, 1):
            for bz in (0, 1):
                attend_near(bx, by, bz)

    stores = []
    split = lax.broadcasted_iota(jnp.int32, (8, 8, 512), 1) < 4
    for bx in (0, 1):
        attended = jnp.concatenate(
            [
                query[bx, :, :, 0, 64 * quad : 64 * quad + 64].reshape(256, 256)
                for quad in (0, 1)
            ],
            axis=1,
        )
        update = jnp.dot(attended, wf_ref[...], preferred_element_type=F32)
        mixed = hidden[bx].reshape(256, 512).astype(F32) + update
        mixed = mixed.reshape(2, 2, 8, 8, 512)
        for by in (0, 1):
            lower, upper = mixed[by, 0], mixed[by, 1]
            even = jnp.where(split, lower, pltpu.roll(upper, 4, 1))
            odd = jnp.where(split, pltpu.roll(lower, 4, 1), upper)
            even = even.reshape(4, 2, 8, 512).astype(BF16)
            odd = odd.reshape(4, 2, 8, 512).astype(BF16)
            for pair in (0, 1):
                out_ref[4 * bx : 4 * bx + 4, 4 * by + 2 * pair] = even[:, pair]
                out_ref[4 * bx : 4 * bx + 4, 4 * by + 2 * pair + 1] = odd[:, pair]
        rows = pl.ds(4 * bx, 4)
        store = pltpu.make_async_copy(out_ref.at[rows], out_hbm.at[rows], store_sem.at[bx])
        store.start()
        stores.append(store)

    for item in rims + faces[0] + faces[1]:
        finish_send(item)
    for store in stores:
        store.wait()


def solution(mesh):
    count_gx = mesh.shape["gx"]
    count_gy = mesh.shape["gy"]

    def body(x, taps, gain, wq, wk, wv, wf, soft, codes, lens):
        hbm = pl.BlockSpec(memory_space=pltpu.HBM)

        def run(*refs):
            kernel(count_gx, count_gy, *refs)

        return pl.pallas_call(
            run,
            out_shape=jax.ShapeDtypeStruct(x.shape, BF16),
            in_specs=[hbm] * 10,
            out_specs=hbm,
            scratch_shapes=[pltpu.VMEM(a.shape, a.dtype) for a in (x, x, taps, gain, wq, wk, wv, wf)]
            + [pltpu.SMEM(a.shape, a.dtype) for a in (soft, codes, lens)]
            + [
                pltpu.VMEM((10, 10, 8, 512), F32),
                pltpu.VMEM((8, 8, 8, 512), F32),
                pltpu.VMEM((2, 8, 8, 512), BF16),
                pltpu.VMEM((2, 8, 8, 512), BF16),
                pltpu.VMEM((4, 8, 512), BF16),
                pltpu.VMEM((2, 2, 2, 4, 16, 512), BF16),
                pltpu.VMEM((2, 2, 2, 4, 16, 512), BF16),
                pltpu.VMEM((2, 2, 2, 4, 16, 512), BF16),
                pltpu.VMEM((2, 2, 2, 4, 16, 512), BF16),
                pltpu.VMEM((2, 2, 2, 2, 256, 256), BF16),
            ]
            + [pltpu.VMEM((2, 2, 2, 64, 512), BF16)] * 6
            + [pltpu.VMEM((2, 2, 2, 64, 512), F32)] * 2
            + [pltpu.SemaphoreType.DMA((count,)) for count in (14, 14, 10, 2)],
            compiler_params=pltpu.CompilerParams(
                collective_id=0, has_side_effects=True, vmem_limit_bytes=60 * 1024 * 1024
            ),
            cost_estimate=pl.CostEstimate(
                flops=4 * 10**9, bytes_accessed=4 * 10**6, transcendentals=2 * 10**6
            ),
        )(x, taps, gain, wq, wk, wv, wf, soft, codes, lens)

    in_specs = (
        P(("slab", "gx"), "gy", None, None),
        P(),
        P(),
        P(),
        P(),
        P(),
        P(),
        P(),
        P(("slab", "gx"), "gy", None, None),
        P(("slab", "gx"), "gy", None),
    )
    out_specs = P(("slab", "gx"), "gy", None, None)
    return jax.shard_map(body, mesh=mesh, in_specs=in_specs, out_specs=out_specs, check_vma=False)
```

profile of v0, /device:TPU:0, one launch (start us, length us, event | category | flops | bytes accessed | tf_op | source)
XLA Modules:
  0.0 22.1 jit_solution(15369959873510565221)
XLA Ops:
  0.0 20.2 %shard_map.100 = bf16[8,8,8,512]{3,2,1,0:T(8,128)(2,1)} custom-call(bf16[8,8,8,512]{3,2,1,0:T(8,128)(2,1)} %refs_0_.1, f32[27,512]{1,0:T(8,128)} %refs_1_.1, f32[512]{0:T(512)} %refs_2_.1, bf16[512,512]{1,0:T(8,128)(2,1)} %refs_3_.1, bf16[512,512]{1,0:T(8,128)(2,1)} %refs_4_.1, bf16[512,512]{1,0:T(8,128)(2,1)} %refs_5_.1, bf16[512,512]{1,0:T(8,128)(2,1)} %refs_6_.1, ...), custom_call_target="tpu_custom_call" | custom-call | flops 4000000000 | bytes 4000000 | tf_op jit(solution)/shard_map/pallas_call | solution.py:476
  20.2 1.9 %copy.12 = bf16[8,8,8,512]{3,2,1,0:T(8,128)(2,1)} copy(bf16[8,8,8,512]{3,2,1,0:T(8,128)(2,1)} %shard_map.100) | data formatting | bytes 1048576
where the time goes:
time: 22.3 us; the launch traced here: 22.1 us
  Pallas kernels  20.2 us (91%)
  local copies, waits for them, and re-layouts  1.87 us (8%)
    pallas_call x1, Pallas kernels, body(): pl.pallas_call(run, out_shape=jax.ShapeDtypeStruct(x.shape, BF16), in_spe...  20.2 us
    unnamed x1, local copies, waits for them, and re-layouts  1.87 us

commit v1 on v0

v1 whole, which is shorter than its diff:
```python
import math

import jax
import jax.numpy as jnp
from jax import lax
from jax.experimental import pallas as pl
from jax.experimental.pallas import tpu as pltpu
from jax.sharding import PartitionSpec as P

BLOCK = 4
MESH = pl.DeviceIdType.MESH
F32 = jnp.float32
BF16 = jnp.bfloat16
X_ROWS = (slice(0, 1), slice(1, 7), slice(7, 8))


def kernel(
    count_gx,
    count_gy,
    x_hbm,
    taps_hbm,
    gain_hbm,
    wq_hbm,
    wk_hbm,
    wv_hbm,
    wf_hbm,
    soft_hbm,
    codes_hbm,
    lens_hbm,
    out_hbm,
    out_ref,
    x_ref,
    taps_ref,
    gain_ref,
    wq_ref,
    wk_ref,
    wv_ref,
    wf_ref,
    soft_ref,
    codes_ref,
    lens_ref,
    framed,
    summed,
    rim_x,
    rim_y,
    rim_c,
    hidden,
    normed,
    near_x,
    near_y,
    query,
    key,
    value,
    key_x,
    value_x,
    key_y,
    value_y,
    attended,
    acc,
    tot,
    send_sem,
    recv_sem,
    load_sem,
    store_sem,
):
    operands = (
        (x_hbm, x_ref),
        (taps_hbm, taps_ref),
        (gain_hbm, gain_ref),
        (wk_hbm, wk_ref),
        (wv_hbm, wv_ref),
        (wq_hbm, wq_ref),
        (soft_hbm, soft_ref),
        (codes_hbm, codes_ref),
        (lens_hbm, lens_ref),
        (wf_hbm, wf_ref),
    )
    loads = [
        pltpu.make_async_copy(src, dst, load_sem.at[i]) for i, (src, dst) in enumerate(operands)
    ]
    for load in loads:
        load.start()
    gx = lax.axis_index("gx")
    gy = lax.axis_index("gy")
    has_x = (gx > 0, gx < count_gx - 1)
    has_y = (gy > 0, gy < count_gy - 1)
    step = (-1, 1)

    def target(dx, dy):
        return {"gx": gx + dx, "gy": gy + dy}

    def exists(dx, dy):
        conds = []
        if dx:
            conds.append(has_x[(dx + 1) // 2])
        if dy:
            conds.append(has_y[(dy + 1) // 2])
        return conds[0] if len(conds) == 1 else conds[0] & conds[1]

    around = [(dx, dy) for dx in (-1, 0, 1) for dy in (-1, 0, 1) if dx or dy]

    barrier = pltpu.get_barrier_semaphore()
    for dx, dy in around:

        @pl.when(exists(dx, dy))
        def _():
            pl.semaphore_signal(barrier, inc=1, device_id=target(dx, dy), device_id_type=MESH)

    span_x = 1 + has_x[0].astype(jnp.int32) + has_x[1].astype(jnp.int32)
    span_y = 1 + has_y[0].astype(jnp.int32) + has_y[1].astype(jnp.int32)
    pl.semaphore_wait(barrier, span_x * span_y - 1)

    def copy(src, dst, out_slot, in_slot, dx, dy):
        return pltpu.make_async_remote_copy(
            src_ref=src,
            dst_ref=dst,
            send_sem=send_sem.at[out_slot],
            recv_sem=recv_sem.at[in_slot],
            device_id=target(dx, dy),
            device_id_type=MESH,
        )

    rims = []
    landing = {}
    for side in (0, 1):
        other = 1 - side
        rims.append((step[side], 0, x_hbm.at[7 * side], rim_x.at[other], side, other))
        landing[side] = (step[side], 0, rim_x.at[side])
    for side in (0, 1):
        for side_y in (0, 1):
            at = 2 * side + side_y
            rims.append(
                (
                    step[side],
                    step[side_y],
                    x_hbm.at[7 * side, 7 * side_y],
                    rim_c.at[3 - at],
                    4 + at,
                    4 + 3 - at,
                )
            )
            landing[4 + at] = (step[side], step[side_y], rim_c.at[at])
    for side in (0, 1):
        other = 1 - side
        rims.append((0, step[side], x_hbm.at[:, 7 * side], rim_y.at[other], 2 + side, 2 + other))
        landing[2 + side] = (0, step[side], rim_y.at[side])

    def face_y(side, at):
        other = 1 - side
        return (
            0,
            step[side],
            normed.at[4 * side + at],
            near_y.at[other, at],
            8 + 4 * side + at,
            8 + 4 * other + at,
        )

    def face_x(side, part):
        other = 1 - side
        rows = X_ROWS[part]
        return (
            step[side],
            0,
            normed.at[rows, side],
            near_x.at[other, rows],
            16 + 3 * side + part,
            16 + 3 * other + part,
        )

    for side in (0, 1):
        for at in range(4):
            landing[8 + 4 * side + at] = (0, step[side], near_y.at[side, at])
        for part in range(3):
            landing[16 + 3 * side + part] = (step[side], 0, near_x.at[side, X_ROWS[part]])

    def start(item):
        dx, dy, src, dst, out_slot, in_slot = item

        @pl.when(exists(dx, dy))
        def _():
            copy(src, dst, out_slot, in_slot, dx, dy).start()

    def finish_send(item):
        dx, dy, src, dst, out_slot, in_slot = item

        @pl.when(exists(dx, dy))
        def _():
            copy(src, dst, out_slot, in_slot, dx, dy).wait_send()

    def arrive(slots, landed, absent=None):
        dx, dy, _ = landing[slots[0]]

        @pl.when(exists(dx, dy))
        def _():
            for slot in slots:
                buffer = landing[slot][2]
                copy(buffer, buffer, slot, slot, dx, dy).wait_recv()
            landed()

        if absent is not None:

            @pl.when(jnp.logical_not(exists(dx, dy)))
            def _():
                absent()

    for item in rims:
        start(item)

    for load in loads[:3]:
        load.wait()

    for at in (0, 9):
        framed[at] = jnp.zeros((10, 8, 512), F32)
        framed[:, at] = jnp.zeros((10, 8, 512), F32)

    @pl.loop(0, 8)
    def _(x):
        framed[1:9, x + 1] = x_ref[x].astype(F32)

    def add_taps(pieces, lanes):
        sums = [None, None, None]
        for a, b, piece in pieces:
            for c in range(3):
                tap = 9 * a + 3 * b + c
                coefficient = taps_ref[tap : tap + 1, lanes]
                if piece.ndim == 3:
                    coefficient = coefficient.reshape(1, 1, 128)
                term = piece * coefficient
                sums[c] = term if sums[c] is None else sums[c] + term
        axis = sums[0].ndim - 2
        depth_at = lax.broadcasted_iota(jnp.int32, sums[0].shape, axis)
        low = jnp.where(depth_at > 0, pltpu.roll(sums[0], 1, axis), 0.0)
        high = jnp.where(depth_at < 7, pltpu.roll(sums[2], 7, axis), 0.0)
        return sums[1] + low + high

    groups = [slice(128 * group, 128 * group + 128) for group in range(4)]

    @pl.loop(0, 8)
    def _(y):
        for lanes in groups:
            pieces = [
                (a, b, framed[y + b, a : a + 8, :, lanes]) for a in range(3) for b in range(3)
            ]
            own = framed[y + 1, 1:9, :, lanes]
            summed[y, :, :, lanes] = own + add_taps(pieces, lanes)

    for side in (0, 1):

        def landed(side=side):
            framed[1:9, 9 * side] = rim_x[side].astype(F32)
            for lanes in groups:
                pieces = [
                    (2 * side, b, framed[b : b + 8, 9 * side, :, lanes]) for b in range(3)
                ]
                before = summed[:, 7 * side, :, lanes]
                summed[:, 7 * side, :, lanes] = before + add_taps(pieces, lanes)

        arrive((side,), landed)

    half_at = lax.broadcasted_iota(jnp.int32, (4, 8, 512), 1) < 4
    gain = gain_ref[...].reshape(1, 1, 512)

    def finish_row(y):
        rows = summed[y].astype(BF16).astype(F32)
        pairs = rows.reshape(4, 2, 8, 512)
        even, odd = pairs[:, 0], pairs[:, 1]
        lower = jnp.where(half_at, even, pltpu.roll(odd, 4, 1))
        upper = jnp.where(half_at, pltpu.roll(even, 4, 1), odd)
        for bz, part in ((0, lower), (1, upper)):
            scale = lax.rsqrt(jnp.mean(part * part, axis=-1, keepdims=True) + 1e-05)
            unit = (part * scale * gain).reshape(2, 16, 512).astype(BF16)
            part = part.reshape(2, 16, 512).astype(BF16)
            for bx in (0, 1):
                hidden[y, bx, bz] = part[bx]
                normed[y, bx, bz] = unit[bx]

    @pl.loop(0, 3)
    def _(i):
        finish_row(1 + i)
        start(face_y(0, 1 + i))
        finish_row(6 - i)
        start(face_y(1, 2 - i))

    for side in (0, 1):
        start(face_x(side, 1))

    for load in loads[3:6]:
        load.wait()
    row = lax.broadcasted_iota(jnp.int32, (256, 256), 0) // 64
    column = lax.broadcasted_iota(jnp.int32, (256, 256), 1) // 64
    same_head = (row == column).astype(F32).astype(BF16)
    head_at = lax.broadcasted_iota(jnp.int32, (64, 256), 1) // 64
    head_of = lax.broadcasted_iota(jnp.int32, (16, 256), 1) // 64

    def units(raw):
        squares = (raw * raw).astype(BF16)
        sums = jnp.dot(squares, same_head, preferred_element_type=F32)
        return raw * lax.rsqrt(sums + 1e-06)

    def project(tokens, w_ref, quad):
        lanes = slice(256 * quad, 256 * quad + 256)
        return jnp.dot(tokens, w_ref[:, lanes], preferred_element_type=F32)

    def gather(parts):
        return jnp.concatenate([part[...].reshape(-1, 512) for part in parts], axis=0)

    def scatter(parts, lanes, values):
        at = 0
        for part in parts:
            shape = part.shape[:-1] + (256,)
            extent = math.prod(part.shape[:-1])
            part[..., lanes] = values[at : at + extent].reshape(shape)
            at += extent

    def keys_values(src, key_dst, value_dst):
        tokens = gather(src)
        for quad in (0, 1):
            lanes = slice(256 * quad, 256 * quad + 256)
            scatter(key_dst, lanes, units(project(tokens, wk_ref, quad)).astype(BF16))
            scatter(value_dst, lanes, project(tokens, wv_ref, quad).astype(BF16))

    def own_rows(spans):
        src = [normed.at[span] for span in spans]
        rows = [y for span in spans for y in range(span.start, span.stop)]
        tokens = gather(src)
        for quad in (0, 1):
            unit = units(project(tokens, wq_ref, quad)).reshape(len(rows), 2, 2, 16, 256)
            for i, y in enumerate(rows):
                by, yi = y // 4, y % 4
                for bx in (0, 1):
                    for bz in (0, 1):
                        for j in range(4):
                            kept = jnp.where(head_of == j, unit[i, bx, bz], 0.0)
                            at = 64 * j + 16 * yi
                            query[bx, by, bz, quad, at : at + 16] = kept.astype(BF16)
        keys_values(src, [key.at[s] for s in spans], [value.at[s] for s in spans])

    own_rows([slice(1, 4), slice(4, 7)])

    def fill(index, ref):
        def landed():
            framed[index] = ref[...].astype(F32)

        return landed

    for side_y in (0, 1):
        at = 9 * side_y
        for side in (0, 1):
            slot = 2 * side + side_y
            arrive((4 + slot,), fill((at, 9 * side), rim_c.at[slot]))
        arrive((2 + side_y,), fill((at, slice(1, 9)), rim_y.at[side_y]))
        y = 7 * side_y
        for lanes in groups:
            pieces = [(a, 2 * side_y, framed[at, a : a + 8, :, lanes]) for a in range(3)]
            summed[y, :, :, lanes] = summed[y, :, :, lanes] + add_taps(pieces, lanes)
        finish_row(y)
        start(face_y(side_y, 3 * side_y))
        for side in (0, 1):
            start(face_x(side, 2 * side_y))

    own_rows([slice(0, 1), slice(7, 8)])

    for load in loads[6:]:
        load.wait()
    log2e = math.log2(math.e)
    slots = codes_ref.shape[3]

    def attend(bx, by, bz, near):
        extent = 64 * len(near)
        slot_at = lax.broadcasted_iota(jnp.int32, (1, extent), 1) // 64
        named = jnp.full((1, extent), -2, jnp.int32)
        for j, (code, _, _) in enumerate(near):
            named = jnp.where(slot_at == j, code, named)
        mask = jnp.zeros((1, extent), F32)
        length = lens_ref[bx, by, bz]
        for s in range(slots):
            code = jnp.where(s < length, codes_ref[bx, by, bz, s], -1)
            mask = jnp.where(named == code, 1.0, mask)
        outs, sums = [], []
        for quad in (0, 1):
            lanes = slice(256 * quad, 256 * quad + 256)
            keys = jnp.concatenate([k[..., lanes].reshape(64, 256) for _, k, _ in near], axis=0)
            values = jnp.concatenate([v[..., lanes].reshape(64, 256) for _, _, v in near], axis=0)
            score = lax.dot_general(
                query[bx, by, bz, quad],
                keys,
                (((1,), (1,)), ((), ())),
                preferred_element_type=F32,
            )
            weights, totals = [], []
            for j in range(4):
                factor = soft_ref[4 * quad + j] * log2e
                weight = jnp.exp2(score[64 * j : 64 * j + 64] * factor) * mask
                totals.append(jnp.sum(weight, axis=-1, keepdims=True))
                weights.append(weight.astype(BF16))
            mixed = jnp.dot(
                jnp.concatenate(weights, axis=0), values, preferred_element_type=F32
            )
            out = mixed[0:64]
            total = jnp.broadcast_to(totals[0], (64, 256))
            for j in range(1, 4):
                out = jnp.where(head_at == j, mixed[64 * j : 64 * j + 64], out)
                total = jnp.where(head_at == j, totals[j], total)
            outs.append(out)
            sums.append(total)
        return outs, sums

    def attend_own(bx, by, bz):
        own, beside = pl.ds(4 * by, 4), pl.ds(4 - 4 * by, 4)
        near = [
            (6 * bz, key.at[own, bx, 0], value.at[own, bx, 0]),
            (5 * (1 - bz), key.at[own, bx, 1], value.at[own, bx, 1]),
            (1 + bx, key.at[own, 1 - bx, bz], value.at[own, 1 - bx, bz]),
            (3 + by, key.at[beside, bx, bz], value.at[beside, bx, bz]),
        ]
        outs, sums = attend(bx, by, bz, near)
        for quad in (0, 1):
            lanes = slice(256 * quad, 256 * quad + 256)
            acc[bx, by, bz, :, lanes] = outs[quad]
            tot[bx, by, bz, :, lanes] = sums[quad]

    for by in (0, 1):
        for bx in (0, 1):
            for bz in (0, 1):
                attend_own(bx, by, bz)

    def clear(*refs):
        def absent():
            for ref in refs:
                ref[...] = jnp.zeros(ref.shape, BF16)

        return absent

    for side in (0, 1):
        arrive(
            tuple(16 + 3 * side + part for part in range(3)),
            lambda side=side: keys_values(
                [near_x.at[side]], [key_x.at[side]], [value_x.at[side]]
            ),
            clear(key_x.at[side], value_x.at[side]),
        )
    for side in (0, 1):
        early = (0, 1, 2) if side == 0 else (1, 2, 3)
        span = slice(early[0], early[-1] + 1)
        arrive(
            tuple(8 + 4 * side + at for at in early),
            lambda side=side, span=span: keys_values(
                [near_y.at[side, span]], [key_y.at[side, span]], [value_y.at[side, span]]
            ),
            clear(key_y.at[side, span], value_y.at[side, span]),
        )
    for side in (0, 1):
        at = 3 - 3 * side
        arrive(
            (8 + 4 * side + at,),
            lambda side=side, at=at: keys_values(
                [near_y.at[side, at]], [key_y.at[side, at]], [value_y.at[side, at]]
            ),
            clear(key_y.at[side, at], value_y.at[side, at]),
        )

    in_x = [has.astype(jnp.int32) for has in has_x]
    in_y = [has.astype(jnp.int32) for has in has_y]

    def attend_near(bx, by, bz):
        rows = pl.ds(4 * by, 4)
        near = [
            (
                jnp.where(in_x[bx] > 0, 2 - bx, -2),
                key_x.at[bx, rows, bz],
                value_x.at[bx, rows, bz],
            ),
            (
                jnp.where(in_y[by] > 0, 4 - by, -2),
                key_y.at[by, :, bx, bz],
                value_y.at[by, :, bx, bz],
            ),
        ]
        outs, sums = attend(bx, by, bz, near)
        for quad in (0, 1):
            lanes = slice(256 * quad, 256 * quad + 256)
            result = (acc[bx, by, bz, :, lanes] + outs[quad]) / (
                tot[bx, by, bz, :, lanes] + sums[quad]
            )
            attended[rows, bx, bz, :, lanes] = result.reshape(4, 16, 256).astype(BF16)

    stores = []
    for by in (0, 1):
        for bx in (0, 1):
            for bz in (0, 1):
                attend_near(bx, by, bz)
        rows = pl.ds(4 * by, 4)
        update = jnp.dot(
            attended[rows].reshape(256, 512), wf_ref[...], preferred_element_type=F32
        )
        mixed = hidden[rows].reshape(256, 512).astype(F32) + update
        mixed = mixed.reshape(4, 2, 2, 2, 8, 512)
        lower = mixed[:, :, 0].reshape(16, 8, 512)
        upper = mixed[:, :, 1].reshape(16, 8, 512)
        split = lax.broadcasted_iota(jnp.int32, (16, 8, 512), 1) < 4
        even = jnp.where(split, lower, pltpu.roll(upper, 4, 1)).astype(BF16)
        odd = jnp.where(split, pltpu.roll(lower, 4, 1), upper).astype(BF16)
        for yi in range(4):
            for pair in range(4):
                out_ref[2 * pair, 4 * by + yi] = even[4 * yi + pair]
                out_ref[2 * pair + 1, 4 * by + yi] = odd[4 * yi + pair]
        store = pltpu.make_async_copy(out_ref.at[:, rows], out_hbm.at[:, rows], store_sem.at[by])
        store.start()
        stores.append(store)

    for item in rims:
        finish_send(item)
    for side in (0, 1):
        for at in range(4):
            finish_send(face_y(side, at))
        for part in range(3):
            finish_send(face_x(side, part))
    for store in stores:
        store.wait()


def solution(mesh):
    count_gx = mesh.shape["gx"]
    count_gy = mesh.shape["gy"]

    def body(x, taps, gain, wq, wk, wv, wf, soft, codes, lens):
        hbm = pl.BlockSpec(memory_space=pltpu.HBM)

        def run(*refs):
            kernel(count_gx, count_gy, *refs)

        return pl.pallas_call(
            run,
            out_shape=jax.ShapeDtypeStruct(x.shape, BF16),
            in_specs=[hbm] * 10,
            out_specs=hbm,
            scratch_shapes=[pltpu.VMEM(a.shape, a.dtype) for a in (x, x, taps, gain, wq, wk, wv, wf)]
            + [pltpu.SMEM(a.shape, a.dtype) for a in (soft, codes, lens)]
            + [
                pltpu.VMEM((10, 10, 8, 512), F32),
                pltpu.VMEM((8, 8, 8, 512), F32),
                pltpu.VMEM((2, 8, 8, 512), BF16),
                pltpu.VMEM((2, 8, 8, 512), BF16),
                pltpu.VMEM((4, 8, 512), BF16),
                pltpu.VMEM((8, 2, 2, 16, 512), BF16),
                pltpu.VMEM((8, 2, 2, 16, 512), BF16),
                pltpu.VMEM((2, 8, 2, 16, 512), BF16),
                pltpu.VMEM((2, 4, 2, 2, 16, 512), BF16),
                pltpu.VMEM((2, 2, 2, 2, 256, 256), BF16),
                pltpu.VMEM((8, 2, 2, 16, 512), BF16),
                pltpu.VMEM((8, 2, 2, 16, 512), BF16),
                pltpu.VMEM((2, 8, 2, 16, 512), BF16),
                pltpu.VMEM((2, 8, 2, 16, 512), BF16),
                pltpu.VMEM((2, 4, 2, 2, 16, 512), BF16),
                pltpu.VMEM((2, 4, 2, 2, 16, 512), BF16),
                pltpu.VMEM((8, 2, 2, 16, 512), BF16),
            ]
            + [pltpu.VMEM((2, 2, 2, 64, 512), F32)] * 2
            + [pltpu.SemaphoreType.DMA((count,)) for count in (22, 22, 10, 2)],
            compiler_params=pltpu.CompilerParams(
                collective_id=0, has_side_effects=True, vmem_limit_bytes=60 * 1024 * 1024
            ),
            cost_estimate=pl.CostEstimate(
                flops=4 * 10**9, bytes_accessed=4 * 10**6, transcendentals=2 * 10**6
            ),
        )(x, taps, gain, wq, wk, wv, wf, soft, codes, lens)

    in_specs = (
        P(("slab", "gx"), "gy", None, None),
        P(),
        P(),
        P(),
        P(),
        P(),
        P(),
        P(),
        P(("slab", "gx"), "gy", None, None),
        P(("slab", "gx"), "gy", None),
    )
    out_specs = P(("slab", "gx"), "gy", None, None)
    return jax.shard_map(body, mesh=mesh, in_specs=in_specs, out_specs=out_specs, check_vma=False)
```

time: 22.3 us -> 19.7 us (0.88)
  the two profiles are of different devices: /device:TPU:0 before, /device:TPU:9 now
where the time goes in v1:
time: 19.7 us; the launch traced here: 19.6 us
  Pallas kernels  17.7 us (90%)
  local copies, waits for them, and re-layouts  1.87 us (9%)
    pallas_call x1, Pallas kernels, body(): pl.pallas_call(run, out_shape=jax.ShapeDtypeStruct(x.shape, BF16), in_spe...  17.7 us
    unnamed x1, local copies, waits for them, and re-layouts  1.87 us

profile of v1, /device:TPU:9, one launch (start us, length us, event | category | flops | bytes accessed | tf_op | source)
XLA Modules:
  0.0 19.6 jit_solution(6638158365107170699)
XLA Ops:
  0.0 17.7 %shard_map.100 = bf16[8,8,8,512]{3,2,1,0:T(8,128)(2,1)} custom-call(bf16[8,8,8,512]{3,2,1,0:T(8,128)(2,1)} %refs_0_.1, f32[27,512]{1,0:T(8,128)} %refs_1_.1, f32[512]{0:T(512)} %refs_2_.1, bf16[512,512]{1,0:T(8,128)(2,1)} %refs_3_.1, bf16[512,512]{1,0:T(8,128)(2,1)} %refs_4_.1, bf16[512,512]{1,0:T(8,128)(2,1)} %refs_5_.1, bf16[512,512]{1,0:T(8,128)(2,1)} %refs_6_.1, ...), custom_call_target="tpu_custom_call" | custom-call | flops 4000000000 | bytes 4000000 | tf_op jit(solution)/shard_map/pallas_call | solution.py:533
  17.7 1.9 %copy.12 = bf16[8,8,8,512]{3,2,1,0:T(8,128)(2,1)} copy(bf16[8,8,8,512]{3,2,1,0:T(8,128)(2,1)} %shard_map.100) | data formatting | bytes 1048576

commit v2 on v1

--- a/solution.py
+++ b/solution.py
@@ -23,19 +23,17 @@
     wq_hbm,
     wk_hbm,
     wv_hbm,
-    wf_hbm,
     soft_hbm,
     codes_hbm,
     lens_hbm,
-    out_hbm,
-    out_ref,
+    hidden,
+    attended,
     x_ref,
     taps_ref,
     gain_ref,
     wq_ref,
     wk_ref,
     wv_ref,
-    wf_ref,
     soft_ref,
     codes_ref,
     lens_ref,
@@ -44,7 +42,6 @@
     rim_x,
     rim_y,
     rim_c,
-    hidden,
     normed,
     near_x,
     near_y,
@@ -55,13 +52,11 @@
     value_x,
     key_y,
     value_y,
-    attended,
     acc,
     tot,
     send_sem,
     recv_sem,
     load_sem,
-    store_sem,
 ):
     operands = (
         (x_hbm, x_ref),
@@ -73,7 +68,6 @@
         (soft_hbm, soft_ref),
         (codes_hbm, codes_ref),
         (lens_hbm, lens_ref),
-        (wf_hbm, wf_ref),
     )
     loads = [
         pltpu.make_async_copy(src, dst, load_sem.at[i]) for i, (src, dst) in enumerate(operands)
@@ -485,11 +479,24 @@
             )
             attended[rows, bx, bz, :, lanes] = result.reshape(4, 16, 256).astype(BF16)
 
-    stores = []
     for by in (0, 1):
         for bx in (0, 1):
             for bz in (0, 1):
                 attend_near(bx, by, bz)
+        rows = pl.ds(4 * by, 4)
+
+    for item in rims:
+        finish_send(item)
+    for side in (0, 1):
+        for at in range(4):
+            finish_send(face_y(side, at))
+        for part in range(3):
+            finish_send(face_x(side, part))
+
+
+def finish(hidden, attended, wf_ref, out_hbm, out_ref, store_sem):
+    stores = []
+    for by in (0, 1):
         rows = pl.ds(4 * by, 4)
         update = jnp.dot(
             attended[rows].reshape(256, 512), wf_ref[...], preferred_element_type=F32
@@ -508,14 +515,6 @@
         store = pltpu.make_async_copy(out_ref.at[:, rows], out_hbm.at[:, rows], store_sem.at[by])
         store.start()
         stores.append(store)
-
-    for item in rims:
-        finish_send(item)
-    for side in (0, 1):
-        for at in range(4):
-            finish_send(face_y(side, at))
-        for part in range(3):
-            finish_send(face_x(side, part))
     for store in stores:
         store.wait()
 
@@ -530,12 +529,16 @@
         def run(*refs):
             kernel(count_gx, count_gy, *refs)
 
-        return pl.pallas_call(
+        x, taps, gain, wq, wk, wv, soft, codes, lens = (
+            pltpu.with_memory_space_constraint(a, pltpu.HBM)
+            for a in (x, taps, gain, wq, wk, wv, soft, codes, lens)
+        )
+        hidden, attended = pl.pallas_call(
             run,
-            out_shape=jax.ShapeDtypeStruct(x.shape, BF16),
-            in_specs=[hbm] * 10,
-            out_specs=hbm,
-            scratch_shapes=[pltpu.VMEM(a.shape, a.dtype) for a in (x, x, taps, gain, wq, wk, wv, wf)]
+            out_shape=[pltpu.VMEM((8, 2, 2, 16, 512), BF16)] * 2,
+            in_specs=[hbm] * 9,
+            out_specs=[pl.BlockSpec(memory_space=pltpu.VMEM)] * 2,
+            scratch_shapes=[pltpu.VMEM(a.shape, a.dtype) for a in (x, taps, gain, wq, wk, wv)]
             + [pltpu.SMEM(a.shape, a.dtype) for a in (soft, codes, lens)]
             + [
                 pltpu.VMEM((10, 10, 8, 512), F32),
@@ -543,7 +546,6 @@
                 pltpu.VMEM((2, 8, 8, 512), BF16),
                 pltpu.VMEM((2, 8, 8, 512), BF16),
                 pltpu.VMEM((4, 8, 512), BF16),
-                pltpu.VMEM((8, 2, 2, 16, 512), BF16),
                 pltpu.VMEM((8, 2, 2, 16, 512), BF16),
                 pltpu.VMEM((2, 8, 2, 16, 512), BF16),
                 pltpu.VMEM((2, 4, 2, 2, 16, 512), BF16),
@@ -554,17 +556,25 @@
                 pltpu.VMEM((2, 8, 2, 16, 512), BF16),
                 pltpu.VMEM((2, 4, 2, 2, 16, 512), BF16),
                 pltpu.VMEM((2, 4, 2, 2, 16, 512), BF16),
-                pltpu.VMEM((8, 2, 2, 16, 512), BF16),
             ]
             + [pltpu.VMEM((2, 2, 2, 64, 512), F32)] * 2
-            + [pltpu.SemaphoreType.DMA((count,)) for count in (22, 22, 10, 2)],
+            + [pltpu.SemaphoreType.DMA((count,)) for count in (22, 22, 9)],
             compiler_params=pltpu.CompilerParams(
-                collective_id=0, has_side_effects=True, vmem_limit_bytes=60 * 1024 * 1024
+                collective_id=0, has_side_effects=True, vmem_limit_bytes=32 * 1024 * 1024
             ),
             cost_estimate=pl.CostEstimate(
                 flops=4 * 10**9, bytes_accessed=4 * 10**6, transcendentals=2 * 10**6
             ),
-        )(x, taps, gain, wq, wk, wv, wf, soft, codes, lens)
+        )(x, taps, gain, wq, wk, wv, soft, codes, lens)
+        vmem = pl.BlockSpec(memory_space=pltpu.VMEM)
+        return pl.pallas_call(
+            finish,
+            out_shape=jax.ShapeDtypeStruct(x.shape, BF16),
+            in_specs=[vmem, vmem, vmem],
+            out_specs=hbm,
+            scratch_shapes=[pltpu.VMEM(x.shape, BF16), pltpu.SemaphoreType.DMA((2,))],
+            compiler_params=pltpu.CompilerParams(vmem_limit_bytes=8 * 1024 * 1024),
+        )(hidden, attended, wf)
 
     in_specs = (
         P(("slab", "gx"), "gy", None, None),

time: 19.7 us -> 17.8 us (0.904)
  local copies, waits for them, and re-layouts: 1.87 us -> 0.01 us
    unnamed x1 -> x2, local copies, waits for them, and re-layouts: 1.87 us -> 0.01 us
    pallas_call x1 -> x2, Pallas kernels: 17.7 us -> 17.6 us  [the longest x1 16.4 us: body(): pl.pallas_call(run, out_shape=[pltpu.VMEM((8, 2, 2, 16, 512), BF16)] * 2,...]
where the time goes in v2:
time: 17.8 us; the launch traced here: 17.6 us
  Pallas kernels  17.6 us (99%)
    pallas_call x1, Pallas kernels, body(): pl.pallas_call(run, out_shape=[pltpu.VMEM((8, 2, 2, 16, 512), BF16)] * 2,...  16.4 us
    pallas_call x1, Pallas kernels, body(): pl.pallas_call(finish, out_shape=jax.ShapeDtypeStruct(x.shape, BF16), in_...  1.18 us

profile of v2, /device:TPU:9, one launch (start us, length us, event | category | flops | bytes accessed | tf_op | source)
XLA Modules:
  0.0 17.6 jit_solution(12812554201627682573)
XLA Ops:
  0.0 0.0 copy-start
  0.0 16.4 %shard_map.100 = (bf16[8,2,2,16,512]{4,3,2,1,0:T(8,128)(2,1)S(1)}, bf16[8,2,2,16,512]{4,3,2,1,0:T(8,128)(2,1)S(1)}) custom-call(bf16[8,8,8,512]{3,2,1,0:T(8,128)(2,1)} %refs_0_.1, f32[27,512]{1,0:T(8,128)} %refs_1_.1, f32[512]{0:T(512)} %refs_2_.1, bf16[512,512]{1,0:T(8,128)(2,1)} %refs_3_.1, bf16[512,512]{1,0:T(8,128)(2,1)} %refs_4_.1, ...), custom_call_target="tpu_custom_call" | custom-call | flops 4000000000 | bytes 4000000 | tf_op jit(solution)/shard_map/pallas_call | solution.py:536
  16.5 0.0 copy-done
  16.5 1.2 %shard_map.101 = bf16[8,8,8,512]{3,2,1,0:T(8,128)(2,1)} custom-call(bf16[8,2,2,16,512]{4,3,2,1,0:T(8,128)(2,1)S(1)} %get-tuple-element.7.hidden, bf16[8,2,2,16,512]{4,3,2,1,0:T(8,128)(2,1)S(1)} %get-tuple-element.8.attended, bf16[512,512]{1,0:T(8,128)(2,1)S(1)} %copy-done), custom_call_target="tpu_custom_call" | custom-call | tf_op jit(solution)/shard_map/pallas_call | solution.py:570
Async XLA Ops:
  0.0 16.5 %copy-start = (bf16[512,512]{1,0:T(8,128)(2,1)S(1)}, bf16[512,512]{1,0:T(8,128)(2,1)}, u32[]{:S(2)}) copy-start(bf16[512,512]{1,0:T(8,128)(2,1)} %wf_ref.1) | copy-start | bytes 1572868

commit v3 on v2

--- a/solution.py
+++ b/solution.py
@@ -139,34 +139,61 @@
         rims.append((0, step[side], x_hbm.at[:, 7 * side], rim_y.at[other], 2 + side, 2 + other))
         landing[2 + side] = (0, step[side], rim_y.at[side])
 
-    def face_y(side, at):
+    early = (slice(0, 3), slice(1, 4))
+    late = (3, 0)
+
+    def face_y(side, at, slot=8):
         other = 1 - side
         return (
             0,
             step[side],
             normed.at[4 * side + at],
             near_y.at[other, at],
-            8 + 4 * side + at,
-            8 + 4 * other + at,
+            8 + side,
+            slot + other,
         )
 
-    def face_x(side, part):
-        other = 1 - side
-        rows = X_ROWS[part]
-        return (
-            step[side],
-            0,
-            normed.at[rows, side],
-            near_x.at[other, rows],
-            16 + 3 * side + part,
-            16 + 3 * other + part,
+    twin = 1 - gx % 2
+    far = gx % 2
+    twin_step = 1 - 2 * far
+    far_x = gx - twin_step
+    has_far = (far_x >= 0) & (far_x < count_gx)
+
+    def face_x(rows):
+        return pltpu.make_async_remote_copy(
+            src_ref=normed.at[rows, far],
+            dst_ref=near_x.at[rows],
+            send_sem=send_sem.at[12],
+            recv_sem=recv_sem.at[12],
+            device_id={"gx": far_x, "gy": gy},
+            device_id_type=MESH,
         )
 
-    for side in (0, 1):
-        for at in range(4):
-            landing[8 + 4 * side + at] = (0, step[side], near_y.at[side, at])
-        for part in range(3):
-            landing[16 + 3 * side + part] = (step[side], 0, near_x.at[side, X_ROWS[part]])
+    def twin_x(rows):
+        return [
+            pltpu.make_async_remote_copy(
+                src_ref=src.at[rows, twin],
+                dst_ref=dst.at[far, rows],
+                send_sem=send_sem.at[13 + i],
+                recv_sem=recv_sem.at[13 + i],
+                device_id={"gx": gx + twin_step, "gy": gy},
+                device_id_type=MESH,
+            )
+            for i, (src, dst) in enumerate(((key, key_x), (value, value_x)))
+        ]
+
+    def start_twin(part):
+        for item in twin_x(X_ROWS[part]):
+            item.start()
+
+    def start_far(part):
+        @pl.when(has_far)
+        def _():
+            face_x(X_ROWS[part]).start()
+
+    for side in (0, 1):
+        landing[8 + side] = (0, step[side], near_y.at[side, early[side]])
+        landing[10 + side] = (0, step[side], near_y.at[side, late[side]])
 
     def start(item):
         dx, dy, src, dst, out_slot, in_slot = item
@@ -177,10 +204,7 @@
 
     def finish_send(item):
         dx, dy, src, dst, out_slot, in_slot = item
-
-        @pl.when(exists(dx, dy))
-        def _():
-            copy(src, dst, out_slot, in_slot, dx, dy).wait_send()
+        copy(src, dst, out_slot, in_slot, dx, dy).wait_send()
 
     def arrive(slots, landed, absent=None):
         dx, dy, _ = landing[slots[0]]
@@ -276,8 +300,7 @@
         finish_row(6 - i)
         start(face_y(1, 2 - i))
 
-    for side in (0, 1):
-        start(face_x(side, 1))
+    start_far(1)
 
     for load in loads[3:6]:
         load.wait()
@@ -331,6 +354,7 @@
         keys_values(src, [key.at[s] for s in spans], [value.at[s] for s in spans])
 
     own_rows([slice(1, 4), slice(4, 7)])
+    start_twin(1)
 
     def fill(index, ref):
         def landed():
@@ -349,11 +373,12 @@
             pieces = [(a, 2 * side_y, framed[at, a : a + 8, :, lanes]) for a in range(3)]
             summed[y, :, :, lanes] = summed[y, :, :, lanes] + add_taps(pieces, lanes)
         finish_row(y)
-        start(face_y(side_y, 3 * side_y))
-        for side in (0, 1):
-            start(face_x(side, 2 * side_y))
+        start(face_y(side_y, 3 * side_y, 10))
+        start_far(2 * side_y)
 
     own_rows([slice(0, 1), slice(7, 8)])
+    start_twin(0)
+    start_twin(2)
 
     for load in loads[6:]:
         load.wait()
@@ -426,33 +451,34 @@
 
         return absent
 
-    for side in (0, 1):
+    @pl.when(has_far)
+    def _():
+        face_x(slice(0, 8)).wait_recv()
+        keys_values([near_x], [key_x.at[far]], [value_x.at[far]])
+
+    @pl.when(jnp.logical_not(has_far))
+    def _():
+        clear(key_x.at[far], value_x.at[far])()
+
+    for side in (0, 1):
+        span = early[side]
         arrive(
-            tuple(16 + 3 * side + part for part in range(3)),
-            lambda side=side: keys_values(
-                [near_x.at[side]], [key_x.at[side]], [value_x.at[side]]
-            ),
-            clear(key_x.at[side], value_x.at[side]),
-        )
-    for side in (0, 1):
-        early = (0, 1, 2) if side == 0 else (1, 2, 3)
-        span = slice(early[0], early[-1] + 1)
-        arrive(
-            tuple(8 + 4 * side + at for at in early),
+            (8 + side,),
             lambda side=side, span=span: keys_values(
                 [near_y.at[side, span]], [key_y.at[side, span]], [value_y.at[side, span]]
             ),
             clear(key_y.at[side, span], value_y.at[side, span]),
         )
     for side in (0, 1):
-        at = 3 - 3 * side
-        arrive(
-            (8 + 4 * side + at,),
-            lambda side=side, at=at: keys_values(
-                [near_y.at[side, at]], [key_y.at[side, at]], [value_y.at[side, at]]
-            ),
-            clear(key_y.at[side, at], value_y.at[side, at]),
-        )
+        arrive((10 + side,), lambda: None, clear(near_y.at[side, late[side]]))
+    keys_values(
+        [near_y.at[side, late[side]] for side in (0, 1)],
+        [key_y.at[side, late[side]] for side in (0, 1)],
+        [value_y.at[side, late[side]] for side in (0, 1)],
+    )
+
+    for item in twin_x(slice(0, 8)):
+        item.wait_recv()
 
     in_x = [has.astype(jnp.int32) for has in has_x]
     in_y = [has.astype(jnp.int32) for has in has_y]
@@ -485,13 +511,29 @@
                 attend_near(bx, by, bz)
         rows = pl.ds(4 * by, 4)
 
-    for item in rims:
-        finish_send(item)
-    for side in (0, 1):
-        for at in range(4):
-            finish_send(face_y(side, at))
-        for part in range(3):
-            finish_send(face_x(side, part))
+    for item in twin_x(slice(0, 8)):
+        item.wait_send()
+
+    @pl.when(has_far)
+    def _():
+        face_x(slice(0, 8)).wait_send()
+
+    for side in (0, 1):
+
+        @pl.when(has_x[side])
+        def _():
+            finish_send(rims[side])
+            for side_y in (0, 1):
+
+                @pl.when(has_y[side_y])
+                def _():
+                    finish_send(rims[2 + 2 * side + side_y])
+
+        @pl.when(has_y[side])
+        def _():
+            finish_send(rims[6 + side])
+            rows = pl.ds(4 * side, 4)
+            finish_send((0, step[side], normed.at[rows], near_y.at[side], 8 + side, 8 + side))
 
 
 def finish(hidden, attended, wf_ref, out_hbm, out_ref, store_sem):
@@ -547,7 +589,7 @@
                 pltpu.VMEM((2, 8, 8, 512), BF16),
                 pltpu.VMEM((4, 8, 512), BF16),
                 pltpu.VMEM((8, 2, 2, 16, 512), BF16),
-                pltpu.VMEM((2, 8, 2, 16, 512), BF16),
+                pltpu.VMEM((8, 2, 16, 512), BF16),
                 pltpu.VMEM((2, 4, 2, 2, 16, 512), BF16),
                 pltpu.VMEM((2, 2, 2, 2, 256, 256), BF16),
                 pltpu.VMEM((8, 2, 2, 16, 512), BF16),
@@ -558,7 +600,7 @@
                 pltpu.VMEM((2, 4, 2, 2, 16, 512), BF16),
             ]
             + [pltpu.VMEM((2, 2, 2, 64, 512), F32)] * 2
-            + [pltpu.SemaphoreType.DMA((count,)) for count in (22, 22, 9)],
+            + [pltpu.SemaphoreType.DMA((count,)) for count in (15, 15, 9)],
             compiler_params=pltpu.CompilerParams(
                 collective_id=0, has_side_effects=True, vmem_limit_bytes=32 * 1024 * 1024
             ),

time: 17.8 us -> 17.2 us (0.966)
  the two profiles are of different devices: /device:TPU:9 before, /device:TPU:1 now
where the time goes in v3:
time: 17.2 us; the launch traced here: 17.1 us
  Pallas kernels  17.1 us (99%)
    pallas_call x1, Pallas kernels, body(): pl.pallas_call(run, out_shape=[pltpu.VMEM((8, 2, 2, 16, 512), BF16)] * 2,...  15.9 us
    pallas_call x1, Pallas kernels, body(): pl.pallas_call(finish, out_shape=jax.ShapeDtypeStruct(x.shape, BF16), in_...  1.18 us

profile of v3, /device:TPU:1, one launch (start us, length us, event | category | flops | bytes accessed | tf_op | source)
XLA Modules:
  0.0 17.1 jit_solution(1559212343022677147)
XLA Ops:
  0.0 0.0 copy-start
  0.0 15.9 %shard_map.100 = (bf16[8,2,2,16,512]{4,3,2,1,0:T(8,128)(2,1)S(1)}, bf16[8,2,2,16,512]{4,3,2,1,0:T(8,128)(2,1)S(1)}) custom-call(bf16[8,8,8,512]{3,2,1,0:T(8,128)(2,1)} %refs_0_.1, f32[27,512]{1,0:T(8,128)} %refs_1_.1, f32[512]{0:T(512)} %refs_2_.1, bf16[512,512]{1,0:T(8,128)(2,1)} %refs_3_.1, bf16[512,512]{1,0:T(8,128)(2,1)} %refs_4_.1, ...), custom_call_target="tpu_custom_call" | custom-call | flops 4000000000 | bytes 4000000 | tf_op jit(solution)/shard_map/pallas_call | solution.py:578
  15.9 0.0 copy-done
  15.9 1.2 %shard_map.101 = bf16[8,8,8,512]{3,2,1,0:T(8,128)(2,1)} custom-call(bf16[8,2,2,16,512]{4,3,2,1,0:T(8,128)(2,1)S(1)} %get-tuple-element.7.hidden, bf16[8,2,2,16,512]{4,3,2,1,0:T(8,128)(2,1)S(1)} %get-tuple-element.8.attended, bf16[512,512]{1,0:T(8,128)(2,1)S(1)} %copy-done), custom_call_target="tpu_custom_call" | custom-call | tf_op jit(solution)/shard_map/pallas_call | solution.py:612
Async XLA Ops:
  0.0 15.9 %copy-start = (bf16[512,512]{1,0:T(8,128)(2,1)S(1)}, bf16[512,512]{1,0:T(8,128)(2,1)}, u32[]{:S(2)}) copy-start(bf16[512,512]{1,0:T(8,128)(2,1)} %wf_ref.1) | copy-start | bytes 1572868

commit v4 on v3

--- a/solution.py
+++ b/solution.py
@@ -11,6 +11,7 @@
 MESH = pl.DeviceIdType.MESH
 F32 = jnp.float32
 BF16 = jnp.bfloat16
+LOG2E = math.log2(math.e)
 X_ROWS = (slice(0, 1), slice(1, 7), slice(7, 8))
 
 
@@ -72,8 +73,6 @@
     loads = [
         pltpu.make_async_copy(src, dst, load_sem.at[i]) for i, (src, dst) in enumerate(operands)
     ]
-    for load in loads:
-        load.start()
     gx = lax.axis_index("gx")
     gy = lax.axis_index("gy")
     has_x = (gx > 0, gx < count_gx - 1)
@@ -91,7 +90,7 @@
             conds.append(has_y[(dy + 1) // 2])
         return conds[0] if len(conds) == 1 else conds[0] & conds[1]
 
-    around = [(dx, dy) for dx in (-1, 0, 1) for dy in (-1, 0, 1) if dx or dy]
+    around = [(-1, 0), (1, 0), (0, -1), (0, 1)]
 
     barrier = pltpu.get_barrier_semaphore()
     for dx, dy in around:
@@ -100,9 +99,9 @@
         def _():
             pl.semaphore_signal(barrier, inc=1, device_id=target(dx, dy), device_id_type=MESH)
 
-    span_x = 1 + has_x[0].astype(jnp.int32) + has_x[1].astype(jnp.int32)
-    span_y = 1 + has_y[0].astype(jnp.int32) + has_y[1].astype(jnp.int32)
-    pl.semaphore_wait(barrier, span_x * span_y - 1)
+    for load in loads[:3]:
+        load.start()
+    pl.semaphore_wait(barrier, sum(has.astype(jnp.int32) for has in has_x + has_y))
 
     def copy(src, dst, out_slot, in_slot, dx, dy):
         return pltpu.make_async_remote_copy(
@@ -125,12 +124,12 @@
             at = 2 * side + side_y
             rims.append(
                 (
-                    step[side],
+                    0,
                     step[side_y],
-                    x_hbm.at[7 * side, 7 * side_y],
-                    rim_c.at[3 - at],
+                    rim_x.at[side, 7 * side_y],
+                    rim_c.at[2 * side + 1 - side_y],
                     4 + at,
-                    4 + 3 - at,
+                    4 + 2 * side + 1 - side_y,
                 )
             )
             landing[4 + at] = (step[side], step[side_y], rim_c.at[at])
@@ -222,8 +221,10 @@
             def _():
                 absent()
 
-    for item in rims:
+    for item in rims[6:] + rims[:2]:
         start(item)
+    for load in loads[3:]:
+        load.start()
 
     for load in loads[:3]:
         load.wait()
@@ -254,28 +255,6 @@
 
     groups = [slice(128 * group, 128 * group + 128) for group in range(4)]
 
-    @pl.loop(0, 8)
-    def _(y):
-        for lanes in groups:
-            pieces = [
-                (a, b, framed[y + b, a : a + 8, :, lanes]) for a in range(3) for b in range(3)
-            ]
-            own = framed[y + 1, 1:9, :, lanes]
-            summed[y, :, :, lanes] = own + add_taps(pieces, lanes)
-
-    for side in (0, 1):
-
-        def landed(side=side):
-            framed[1:9, 9 * side] = rim_x[side].astype(F32)
-            for lanes in groups:
-                pieces = [
-                    (2 * side, b, framed[b : b + 8, 9 * side, :, lanes]) for b in range(3)
-                ]
-                before = summed[:, 7 * side, :, lanes]
-                summed[:, 7 * side, :, lanes] = before + add_taps(pieces, lanes)
-
-        arrive((side,), landed)
-
     half_at = lax.broadcasted_iota(jnp.int32, (4, 8, 512), 1) < 4
     gain = gain_ref[...].reshape(1, 1, 512)
 
@@ -293,22 +272,103 @@
                 hidden[y, bx, bz] = part[bx]
                 normed[y, bx, bz] = unit[bx]
 
-    @pl.loop(0, 3)
-    def _(i):
-        finish_row(1 + i)
-        start(face_y(0, 1 + i))
-        finish_row(6 - i)
-        start(face_y(1, 2 - i))
-
+    def finish_half(y, h):
+        rows = summed[y, pl.ds(4 * h, 4)].astype(BF16).astype(F32)
+        pairs = rows.reshape(2, 2, 8, 512)
+        even, odd = pairs[:, 0], pairs[:, 1]
+        first = half_at[:2]
+        lower = jnp.where(first, even, pltpu.roll(odd, 4, 1))
+        upper = jnp.where(first, pltpu.roll(even, 4, 1), odd)
+        for bz, part in ((0, lower), (1, upper)):
+            scale = lax.rsqrt(jnp.mean(part * part, axis=-1, keepdims=True) + 1e-05)
+            hidden[y, h, bz] = part.reshape(16, 512).astype(BF16)
+            normed[y, h, bz] = (part * scale * gain).reshape(16, 512).astype(BF16)
+
+    def convolve_half(h):
+        @pl.loop(0, 3)
+        def _(i):
+            y = 1 + 2 * i
+            for lanes in groups:
+                pieces = []
+                for a in range(3):
+                    for b in range(3):
+                        piece = framed[pl.ds(y + b, 2), pl.ds(4 * h + a, 4), :, lanes]
+                        pieces.append((a, b, piece.reshape(8, 8, 128)))
+                own = framed[pl.ds(y + 1, 2), pl.ds(4 * h + 1, 4), :, lanes]
+                result = own + add_taps(pieces, lanes).reshape(2, 4, 8, 128)
+                summed[pl.ds(y, 2), pl.ds(4 * h, 4), :, lanes] = result
+
+    def convolve_ends():
+        @pl.loop(0, 2)
+        def _(i):
+            y = 7 * i
+            for lanes in groups:
+                pieces = [
+                    (a, b, framed[y + b, a : a + 8, :, lanes]) for a in range(3) for b in range(3)
+                ]
+                own = framed[y + 1, 1:9, :, lanes]
+                summed[y, :, :, lanes] = own + add_taps(pieces, lanes)
+
+    def add_rim(side, first, last):
+        dx, dy, buffer = landing[side]
+        copy(buffer, buffer, side, side, dx, dy).wait_recv()
+        for item in rims[2 + 2 * side : 4 + 2 * side]:
+            start(item)
+        framed[1:9, 9 * side] = rim_x[side].astype(F32)
+        for lanes in groups:
+            pieces = [(2 * side, b, framed[first + b : last + b, 9 * side, :, lanes]) for b in range(3)]
+            before = summed[first:last, 7 * side, :, lanes]
+            summed[first:last, 7 * side, :, lanes] = before + add_taps(pieces, lanes)
+
+    for h, first, last in ((twin, 1, 7), (far, 0, 8)):
+        convolve_half(h)
+        if first == 0:
+            pl.when(has_far)(convolve_ends)
+        for side in (0, 1):
+
+            @pl.when((h == side) & has_x[side])
+            def _():
+                add_rim(side, first, last)
+
+        for toward in (0, 1):
+            other = 1 - toward
+
+            @pl.loop(1 + 3 * toward, 4 + 3 * toward)
+            def _(y):
+                finish_half(y, h)
+
+            rows = slice(1 + 3 * toward, 4 + 3 * toward)
+            start(
+                (
+                    0,
+                    step[toward],
+                    normed.at[rows, h],
+                    near_y.at[other, early[other], h],
+                    8 + toward,
+                    8 + other,
+                )
+            )
     start_far(1)
 
-    for load in loads[3:6]:
+    @pl.when(jnp.logical_not(has_far))
+    def _():
+        convolve_ends()
+
+    for load in loads[3:]:
         load.wait()
     row = lax.broadcasted_iota(jnp.int32, (256, 256), 0) // 64
     column = lax.broadcasted_iota(jnp.int32, (256, 256), 1) // 64
     same_head = (row == column).astype(F32).astype(BF16)
     head_at = lax.broadcasted_iota(jnp.int32, (64, 256), 1) // 64
     head_of = lax.broadcasted_iota(jnp.int32, (16, 256), 1) // 64
+    heads = [(head_of == j).astype(F32).astype(BF16) for j in range(4)]
+    lane_head = lax.broadcasted_iota(jnp.int32, (1, 256), 1) // 64
+    factors = []
+    for quad in (0, 1):
+        factor = jnp.zeros((1, 256), F32)
+        for j in range(4):
+            factor = jnp.where(lane_head == j, soft_ref[4 * quad + j] * LOG2E, factor)
+        factors.append(factor)
 
     def units(raw):
         squares = (raw * raw).astype(BF16)
@@ -342,16 +402,18 @@
         rows = [y for span in spans for y in range(span.start, span.stop)]
         tokens = gather(src)
         for quad in (0, 1):
-            unit = units(project(tokens, wq_ref, quad)).reshape(len(rows), 2, 2, 16, 256)
+            unit = units(project(tokens, wq_ref, quad)) * factors[quad]
+            unit = unit.astype(BF16).reshape(len(rows), 2, 2, 16, 256)
             for i, y in enumerate(rows):
                 by, yi = y // 4, y % 4
                 for bx in (0, 1):
                     for bz in (0, 1):
                         for j in range(4):
-                            kept = jnp.where(head_of == j, unit[i, bx, bz], 0.0)
+                            kept = unit[i, bx, bz] * heads[j]
                             at = 64 * j + 16 * yi
-                            query[bx, by, bz, quad, at : at + 16] = kept.astype(BF16)
+                            query[bx, by, bz, quad, at : at + 16] = kept
         keys_values(src, [key.at[s] for s in spans], [value.at[s] for s in spans])
+
 
     own_rows([slice(1, 4), slice(4, 7)])
     start_twin(1)
@@ -380,9 +442,6 @@
     start_twin(0)
     start_twin(2)
 
-    for load in loads[6:]:
-        load.wait()
-    log2e = math.log2(math.e)
     slots = codes_ref.shape[3]
 
     def attend(bx, by, bz, near):
@@ -409,8 +468,7 @@
             )
             weights, totals = [], []
             for j in range(4):
-                factor = soft_ref[4 * quad + j] * log2e
-                weight = jnp.exp2(score[64 * j : 64 * j + 64] * factor) * mask
+                weight = jnp.exp2(score[64 * j : 64 * j + 64]) * mask
                 totals.append(jnp.sum(weight, axis=-1, keepdims=True))
                 weights.append(weight.astype(BF16))
             mixed = jnp.dot(
@@ -451,15 +509,6 @@
 
         return absent
 
-    @pl.when(has_far)
-    def _():
-        face_x(slice(0, 8)).wait_recv()
-        keys_values([near_x], [key_x.at[far]], [value_x.at[far]])
-
-    @pl.when(jnp.logical_not(has_far))
-    def _():
-        clear(key_x.at[far], value_x.at[far])()
-
     for side in (0, 1):
         span = early[side]
         arrive(
@@ -469,6 +518,15 @@
             ),
             clear(key_y.at[side, span], value_y.at[side, span]),
         )
+    @pl.when(has_far)
+    def _():
+        face_x(slice(0, 8)).wait_recv()
+        keys_values([near_x], [key_x.at[far]], [value_x.at[far]])
+
+    @pl.when(jnp.logical_not(has_far))
+    def _():
+        clear(key_x.at[far], value_x.at[far])()
+
     for side in (0, 1):
         arrive((10 + side,), lambda: None, clear(near_y.at[side, late[side]]))
     keys_values(
@@ -538,23 +596,25 @@
 
 def finish(hidden, attended, wf_ref, out_hbm, out_ref, store_sem):
     stores = []
-    for by in (0, 1):
-        rows = pl.ds(4 * by, 4)
+    split = lax.broadcasted_iota(jnp.int32, (8, 8, 512), 1) < 4
+    for part in range(4):
+        rows = pl.ds(2 * part, 2)
         update = jnp.dot(
-            attended[rows].reshape(256, 512), wf_ref[...], preferred_element_type=F32
+            attended[rows].reshape(128, 512), wf_ref[...], preferred_element_type=F32
         )
-        mixed = hidden[rows].reshape(256, 512).astype(F32) + update
-        mixed = mixed.reshape(4, 2, 2, 2, 8, 512)
-        lower = mixed[:, :, 0].reshape(16, 8, 512)
-        upper = mixed[:, :, 1].reshape(16, 8, 512)
-        split = lax.broadcasted_iota(jnp.int32, (16, 8, 512), 1) < 4
+        mixed = hidden[rows].reshape(128, 512).astype(F32) + update
+        mixed = mixed.reshape(2, 2, 2, 2, 8, 512)
+        lower = mixed[:, :, 0].reshape(8, 8, 512)
+        upper = mixed[:, :, 1].reshape(8, 8, 512)
         even = jnp.where(split, lower, pltpu.roll(upper, 4, 1)).astype(BF16)
         odd = jnp.where(split, pltpu.roll(lower, 4, 1), upper).astype(BF16)
-        for yi in range(4):
+        for yi in range(2):
             for pair in range(4):
-                out_ref[2 * pair, 4 * by + yi] = even[4 * yi + pair]
-                out_ref[2 * pair + 1, 4 * by + yi] = odd[4 * yi + pair]
-        store = pltpu.make_async_copy(out_ref.at[:, rows], out_hbm.at[:, rows], store_sem.at[by])
+                out_ref[2 * pair, 2 * part + yi] = even[4 * yi + pair]
+                out_ref[2 * pair + 1, 2 * part + yi] = odd[4 * yi + pair]
+        store = pltpu.make_async_copy(
+            out_ref.at[:, rows], out_hbm.at[:, rows], store_sem.at[part]
+        )
         store.start()
         stores.append(store)
     for store in stores:
@@ -614,7 +674,7 @@
             out_shape=jax.ShapeDtypeStruct(x.shape, BF16),
             in_specs=[vmem, vmem, vmem],
             out_specs=hbm,
-            scratch_shapes=[pltpu.VMEM(x.shape, BF16), pltpu.SemaphoreType.DMA((2,))],
+            scratch_shapes=[pltpu.VMEM(x.shape, BF16), pltpu.SemaphoreType.DMA((4,))],
             compiler_params=pltpu.CompilerParams(vmem_limit_bytes=8 * 1024 * 1024),
         )(hidden, attended, wf)
 

time: 17.2 us -> 16.8 us (0.977)
  Pallas kernels: 17.1 us -> 16.6 us
    pallas_call x1, Pallas kernels: 15.9 us -> 15.5 us  [body(): pl.pallas_call(run, out_shape=[pltpu.VMEM((8, 2, 2, 16, 512), BF16)] * 2,...]
where the time goes in v4:
time: 16.8 us; the launch traced here: 16.6 us
  Pallas kernels  16.6 us (99%)
    pallas_call x1, Pallas kernels, body(): pl.pallas_call(run, out_shape=[pltpu.VMEM((8, 2, 2, 16, 512), BF16)] * 2,...  15.5 us
    pallas_call x1, Pallas kernels, body(): pl.pallas_call(finish, out_shape=jax.ShapeDtypeStruct(x.shape, BF16), in_...  1.15 us

profile of v4, /device:TPU:1, one launch (start us, length us, event | category | flops | bytes accessed | tf_op | source)
XLA Modules:
  0.0 16.6 jit_solution(5837197802726056893)
XLA Ops:
  0.0 0.0 copy-start
  0.0 15.5 %shard_map.100 = (bf16[8,2,2,16,512]{4,3,2,1,0:T(8,128)(2,1)S(1)}, bf16[8,2,2,16,512]{4,3,2,1,0:T(8,128)(2,1)S(1)}) custom-call(bf16[8,8,8,512]{3,2,1,0:T(8,128)(2,1)} %refs_0_.1, f32[27,512]{1,0:T(8,128)} %refs_1_.1, f32[512]{0:T(512)} %refs_2_.1, bf16[512,512]{1,0:T(8,128)(2,1)} %refs_3_.1, bf16[512,512]{1,0:T(8,128)(2,1)} %refs_4_.1, ...), custom_call_target="tpu_custom_call" | custom-call | flops 4000000000 | bytes 4000000 | tf_op jit(solution)/shard_map/pallas_call | solution.py:638
  15.5 0.0 copy-done
  15.5 1.1 %shard_map.101 = bf16[8,8,8,512]{3,2,1,0:T(8,128)(2,1)} custom-call(bf16[8,2,2,16,512]{4,3,2,1,0:T(8,128)(2,1)S(1)} %get-tuple-element.7.hidden, bf16[8,2,2,16,512]{4,3,2,1,0:T(8,128)(2,1)S(1)} %get-tuple-element.8.attended, bf16[512,512]{1,0:T(8,128)(2,1)S(1)} %copy-done), custom_call_target="tpu_custom_call" | custom-call | tf_op jit(solution)/shard_map/pallas_call | solution.py:672
Async XLA Ops:
  0.0 15.5 %copy-start = (bf16[512,512]{1,0:T(8,128)(2,1)S(1)}, bf16[512,512]{1,0:T(8,128)(2,1)}, u32[]{:S(2)}) copy-start(bf16[512,512]{1,0:T(8,128)(2,1)} %wf_ref.1) | copy-start | bytes 1572868

commit v5 on v4

--- a/solution.py
+++ b/solution.py
@@ -221,7 +221,7 @@
             def _():
                 absent()
 
-    for item in rims[6:] + rims[:2]:
+    for item in rims[:2] + rims[6:]:
         start(item)
     for load in loads[3:]:
         load.start()
@@ -371,7 +371,8 @@
         factors.append(factor)
 
     def units(raw):
-        squares = (raw * raw).astype(BF16)
+        rounded = raw.astype(BF16)
+        squares = rounded * rounded
         sums = jnp.dot(squares, same_head, preferred_element_type=F32)
         return raw * lax.rsqrt(sums + 1e-06)
 
@@ -558,9 +559,10 @@
         outs, sums = attend(bx, by, bz, near)
         for quad in (0, 1):
             lanes = slice(256 * quad, 256 * quad + 256)
-            result = (acc[bx, by, bz, :, lanes] + outs[quad]) / (
-                tot[bx, by, bz, :, lanes] + sums[quad]
-            )
+            total = tot[bx, by, bz, :, lanes] + sums[quad]
+            inverse = pl.reciprocal(total, approx=True)
+            inverse = inverse * (2.0 - total * inverse)
+            result = (acc[bx, by, bz, :, lanes] + outs[quad]) * inverse
             attended[rows, bx, bz, :, lanes] = result.reshape(4, 16, 256).astype(BF16)
 
     for by in (0, 1):

time: 16.8 us -> 16.8 us (level)
  no operation moved by 1% of the time
where the time goes in v5:
time: 16.8 us; the launch traced here: 16.6 us
  Pallas kernels  16.6 us (99%)
    pallas_call x1, Pallas kernels, body(): pl.pallas_call(run, out_shape=[pltpu.VMEM((8, 2, 2, 16, 512), BF16)] * 2,...  15.5 us
    pallas_call x1, Pallas kernels, body(): pl.pallas_call(finish, out_shape=jax.ShapeDtypeStruct(x.shape, BF16), in_...  1.15 us

profile of v5, /device:TPU:1, one launch (start us, length us, event | category | flops | bytes accessed | tf_op | source)
XLA Modules:
  0.0 16.6 jit_solution(16216137887633819946)
XLA Ops:
  0.0 0.0 copy-start
  0.0 15.5 %shard_map.100 = (bf16[8,2,2,16,512]{4,3,2,1,0:T(8,128)(2,1)S(1)}, bf16[8,2,2,16,512]{4,3,2,1,0:T(8,128)(2,1)S(1)}) custom-call(bf16[8,8,8,512]{3,2,1,0:T(8,128)(2,1)} %refs_0_.1, f32[27,512]{1,0:T(8,128)} %refs_1_.1, f32[512]{0:T(512)} %refs_2_.1, bf16[512,512]{1,0:T(8,128)(2,1)} %refs_3_.1, bf16[512,512]{1,0:T(8,128)(2,1)} %refs_4_.1, ...), custom_call_target="tpu_custom_call" | custom-call | flops 4000000000 | bytes 4000000 | tf_op jit(solution)/shard_map/pallas_call | solution.py:640
  15.5 0.0 copy-done
  15.5 1.2 %shard_map.101 = bf16[8,8,8,512]{3,2,1,0:T(8,128)(2,1)} custom-call(bf16[8,2,2,16,512]{4,3,2,1,0:T(8,128)(2,1)S(1)} %get-tuple-element.7.hidden, bf16[8,2,2,16,512]{4,3,2,1,0:T(8,128)(2,1)S(1)} %get-tuple-element.8.attended, bf16[512,512]{1,0:T(8,128)(2,1)S(1)} %copy-done), custom_call_target="tpu_custom_call" | custom-call | tf_op jit(solution)/shard_map/pallas_call | solution.py:674
Async XLA Ops:
  0.0 15.5 %copy-start = (bf16[512,512]{1,0:T(8,128)(2,1)S(1)}, bf16[512,512]{1,0:T(8,128)(2,1)}, u32[]{:S(2)}) copy-start(bf16[512,512]{1,0:T(8,128)(2,1)} %wf_ref.1) | copy-start | bytes 1572868
